TPU v7x, 256 devices: a whole 4x4x8 slice. The times are simulated.
256 devices in a mesh: blk: 16 (over x_lo, y, core), uly: 16 (over x_hi, z).
Axes of the slice: x: 4 (x_hi: 2, x_lo: 2; x = x_hi * 2 + x_lo), y: 4, z: 8, core: 2. Of those that a mesh axis runs over, the one named last changes fastest.
Arguments:
- query_states: bfloat16 [16384, 8192], P(('blk', 'uly')), may hold values from -16 to 16
- key_states: bfloat16 [16384, 512], P(('blk', 'uly')), may hold values from -6 to 6
- value_states: bfloat16 [16384, 512], P(('blk', 'uly')), may hold values from -6 to 6
- attn_output: bfloat16 [16384, 8192], P(('blk', 'uly')), may hold values from -6 to 6
- grad_output: bfloat16 [16384, 8192], P(('blk', 'uly')), may hold values from -6 to 6
- token_pos: int32 [16384], P(('blk', 'uly')), may hold values from 0 to 16383, as said below
Outputs:
- grad_query: bfloat16 [16384, 8192], P(('blk', 'uly'))
- grad_key: bfloat16 [16384, 512], P(('blk', 'uly'))
- grad_value: bfloat16 [16384, 512], P(('blk', 'uly'))
Inputs may be any that keep to these rules, and one draw needn't show every extreme that they name: `token_pos`: token rows form 32 runs of 512 consecutive rows; run c holds the positions p(c) * 512 to p(c) * 512 + 511 in rising order, where p is a permutation of the runs.
All inputs are finite; a program needn't handle non-finite values.
Results may differ from a plain program's by a relative error of at most 0.005.
Values may be sent and summed in bfloat16 or wider, within the bound.
A program may use at most 128 MiB of HBM per device.

v0:
```python
import functools

import jax
import jax.numpy as jnp
from jax import lax
from jax.experimental import pallas as pl
from jax.experimental.pallas import tpu as pltpu
from jax.sharding import PartitionSpec as P

MESH = pl.DeviceIdType.MESH
B16 = jnp.bfloat16
F32 = jnp.float32
QH, KVH, HD = 64, 4, 128
G = QH // KVH
T = 64
NZ = 8
R = G * T
NK = 2048
HALF = NK // 2
PREV, OWN = 0, 1
SCALE = HD ** -0.5
LOG2E = 1.4426950408889634
HIDE = -1e30
C1 = 256
NT = (((1,), (1,)), ((), ()))
NN = (((1,), (0,)), ((), ()))
ORDER = (4, 3, 5, 2, 6, 1, 7, 0)


def dot(a, b, dims=NN):
    return lax.dot_general(a, b, dims, preferred_element_type=F32)


def kernel(nblk, q_hbm, g_hbm, o_hbm, k_ref, v_ref, pos_ref, dq_hbm, dk_ref, dv_ref,
           q_v, g_v, o_v, dq_v, kv, posb, mk, qa, ga, ds_sc, p_sc, sc, m_sc, l_sc,
           acc, sp_p, rp_p, s_a1, s_a2, r_a1, r_a2, s_b, r_b,
           in_sem, out_sem, gx_s, gx_r, gu_s, gu_r, gd_s, gd_r, gn_s, gn_r, ga_s, gb_s, gc_s, g_r, gc_r, px_s, px_r, pb_s, pb_r,
           rp_s, rp_r, ra_s, ra_r, rb_s, rb_r):
    b = lax.axis_index("blk")
    u = lax.axis_index("uly")
    z = lax.rem(u, NZ)
    xh = u // NZ
    def at(other, step):
        return (b, (1 - xh if other else xh) * NZ + lax.rem(z + step + NZ, NZ))

    near = [at(x, i) for x in (0, 1) for i in (0, 1, -1, 2, -2)][1:]
    xp = at(1, 0)
    nx = (lax.rem(b + 1, nblk), u)
    pb = (lax.rem(b + nblk - 1, nblk), u)

    def rcopy(src, dst, ss, rs, dev):
        return pltpu.make_async_remote_copy(src_ref=src, dst_ref=dst, send_sem=ss, recv_sem=rs,
                                            device_id=dev, device_id_type=MESH)

    loads = [pltpu.make_async_copy(a, c, in_sem.at[i])
             for i, (a, c) in enumerate(((q_hbm, q_v), (g_hbm, g_v), (o_hbm, o_v)))]
    for c in loads:
        c.start()
    for h in range(KVH):
        kv[h, OWN, 0, 0, 0] = k_ref[:, h * HD:(h + 1) * HD]
        kv[h, OWN, 1, 0, 0] = v_ref[:, h * HD:(h + 1) * HD]
    base = jnp.min(pos_ref[...], axis=1, keepdims=True) - T * z
    posb[OWN, 0] = jnp.broadcast_to(base, (8, 128))

    barrier = pltpu.get_barrier_semaphore()
    for dev in near + [nx, pb]:
        pl.semaphore_signal(barrier, inc=1, device_id=dev, device_id_type=MESH)
    pl.semaphore_wait(barrier, 11)

    def g_a(i):
        own = kv.at[0, OWN, i, 0, 0]
        out = [rcopy(own, kv.at[0, OWN, i, 0, 1], ga_s.at[i, 0], g_r.at[i, 0], xp)]
        for n, step in enumerate((2, -2, 1, -1)):
            for x in range(2):
                d = (NZ - step) % NZ
                out.append(rcopy(own, kv.at[0, OWN, i, d, x], ga_s.at[i, 1 + 2 * n + x], g_r.at[i, d], at(x, step)))
        return out

    def g_b(i):
        lo, hi = kv.at[0, OWN, i, 6], kv.at[0, OWN, i, 2]
        return [rcopy(lo, kv.at[0, OWN, i, 5], gb_s.at[i, 0], g_r.at[i, 5], at(0, 1)),
                rcopy(hi, kv.at[0, OWN, i, 3], gb_s.at[i, 1], g_r.at[i, 3], at(0, -1)),
                rcopy((lo, hi)[i], kv.at[0, OWN, i, 4], gb_s.at[i, 2], g_r.at[i, 4], at(0, (2, -2)[i]))]

    def g_c(i, n):
        part = (slice(0, 3), slice(6, 8), slice(3, 6))[n]
        return rcopy(kv.at[0, OWN, i, part], kv.at[0, PREV, i, part], gc_s.at[i, n], gc_r.at[i, n], nx)

    def g_wait(i, d):
        ref = kv.at[0, OWN, i, 0, 1] if d == 0 else kv.at[0, OWN, i, d]
        tag = (gb_s if d in (3, 4, 5) else ga_s).at[i, 0]
        rcopy(ref, ref, tag, g_r.at[i, d], xp).wait_recv()

    def gather_send(i):
        for c in g_a(i):
            c.start()

    def gather_relay(i):
        g_wait(i, 6)
        g_wait(i, 2)
        for c in g_b(i):
            c.start()

    def gather_near(i):
        for d in (0, 1, 7):
            g_wait(i, d)
        g_c(i, 0).start()
        g_c(i, 1).start()

    def gather_last(i):
        for d in (3, 4, 5):
            g_wait(i, d)
        g_c(i, 2).start()

    def gx(h):
        return rcopy(kv.at[h, OWN, :, 0, 0], kv.at[h, OWN, :, 0, 1], gx_s.at[h], gx_r.at[h], xp)

    def gu(h, s):
        src = (NZ - s) % NZ
        if s < 3:
            return rcopy(kv.at[h, OWN, :, src], kv.at[h, OWN, :, src - 1 if src else NZ - 1], gu_s.at[h, s], gu_r.at[h, s], at(0, 1))
        return rcopy(kv.at[h, OWN, 0, 5], kv.at[h, OWN, 0, 4], gu_s.at[h, s], gu_r.at[h, s], at(0, 1))

    def gd(h, s):
        if s < 3:
            return rcopy(kv.at[h, OWN, :, s], kv.at[h, OWN, :, s + 1], gd_s.at[h, s], gd_r.at[h, s], at(0, -1))
        return rcopy(kv.at[h, OWN, 1, 3], kv.at[h, OWN, 1, 4], gd_s.at[h, s], gd_r.at[h, s], at(0, -1))

    def gn(h, d):
        return rcopy(kv.at[h, OWN, :, d], kv.at[h, PREV, :, d], gn_s.at[h], gn_r.at[h], nx)

    def gn_all(h):
        return rcopy(kv.at[h, OWN], kv.at[h, PREV], gn_s.at[h], gn_r.at[h], nx)

    def ring(h, s):
        if h >= KVH:
            return
        if s == 0:
            gx(h).wait_recv()
            gu(h, 0).start()
            gd(h, 0).start()
            gn(h, 0).start()
            return
        gu(h, s - 1).wait_recv()
        if s < 4:
            gu(h, s).start()
        gd(h, s - 1).wait_recv()
        if s < 4:
            gd(h, s).start()
            gn(h, NZ - s).start()
        gn(h, s).start()

    def pos_x():
        return rcopy(posb.at[OWN, 0], posb.at[OWN, 1], px_s, px_r, xp)

    def pos_b():
        return rcopy(posb.at[OWN], posb.at[PREV], pb_s, pb_r, nx)

    gather_send(0)
    pos_x().start()
    for h in range(1, KVH):
        gx(h).start()

    lane = lax.broadcasted_iota(jnp.int32, (T, 128), 1)
    row = lax.broadcasted_iota(jnp.int32, (T, 128), 0)
    eye = jnp.where(lane == row, 1.0, 0.0).astype(B16)
    ones = jnp.where(lax.broadcasted_iota(jnp.int32, (256, 128), 1) < 3, 1.0, 0.0).astype(B16)
    for g in range(G):
        for h in range(KVH):
            qa[h, g * T:(g + 1) * T, HD:] = eye

    for c in loads:
        c.wait()

    def prep_rows(h):
        for g in range(G):
            sl = pl.ds(h * (G * HD) + g * HD if isinstance(h, int) else pl.multiple_of(h * (G * HD) + g * HD, HD), HD)
            rs = pl.ds(g * T, T)
            qa[h, rs, :HD] = q_v[:, sl]
            gg = g_v[:, sl]
            ga[h, rs, :HD] = gg
            d = -jnp.sum(gg.astype(F32) * o_v[:, sl].astype(F32), axis=1, keepdims=True)
            d1 = d.astype(B16)
            e = d - d1.astype(F32)
            d2 = e.astype(B16)
            d3 = e - d2.astype(F32)
            ga[h, rs, HD:] = jnp.where(lane == 0, d1.astype(F32), jnp.where(lane == 1, d2.astype(F32), jnp.where(lane == 2, d3, 0.0))).astype(B16)

    def make_mask(s):
        for d in range(NZ):
            first = T * lax.rem(z + d, NZ)
            for x in range(2):
                kp = posb[s, x, 0:1, :] + first + row
                qp = posb[OWN, 0, 0:1, :] + T * z + lane
                mk[pl.ds(s * HALF + d * 128 + x * T, T), :] = jnp.where(kp <= qp, 0.0, HIDE).astype(B16)

    def r_p(h, d):
        return rcopy(sp_p.at[h, d], rp_p.at[h, d], rp_s.at[h, d], rp_r.at[h, d], pb)

    def r_a(h):
        return [rcopy(s_a2.at[h, 0], r_a2.at[h, 0], ra_s.at[h, 2], ra_r.at[h, 2], at(0, 2)),
                rcopy(s_a2.at[h, 1], r_a2.at[h, 1], ra_s.at[h, 3], ra_r.at[h, 3], at(0, -2)),
                rcopy(s_a1.at[h, 0], r_a1.at[h, 0], ra_s.at[h, 0], ra_r.at[h, 0], at(0, 1)),
                rcopy(s_a1.at[h, 1], r_a1.at[h, 1], ra_s.at[h, 1], ra_r.at[h, 1], at(0, -1))]

    def r_b_copy(h, i, x):
        step = (2, -2, 1, -1, 0)[i]
        return rcopy(s_b.at[h, i, x], r_b.at[h, i, x], rb_s.at[h, i, x], rb_r.at[h, i], at(x, step))

    def term(h, d, i):
        return acc[h, d, i] + rp_p[h, d, i].astype(F32)

    def reduce_first(h):
        for d in (4, 3, 5):
            r_p(h, d).wait_recv()
        for i in range(2):
            s_a2[h, i] = term(h, 4, i).astype(B16)
            s_a1[h, 0, i] = term(h, 3, i).astype(B16)
            s_a1[h, 1, i] = term(h, 5, i).astype(B16)
        for c in r_a(h):
            c.start()

    def reduce_relay(h):
        for d in (1, 7, 0):
            r_p(h, d).wait_recv()
        for j, d in ((2, 1), (3, 7), (4, 0)):
            for i in range(2):
                t = term(h, d, i)
                if j == 4:
                    acc[h, 0, i] = t
                    s_b[h, j, 1, i] = t[T:].astype(B16)
                else:
                    s_b[h, j, 0, i] = t[:T].astype(B16)
                    s_b[h, j, 1, i] = t[T:].astype(B16)
        for j in (2, 3, 4):
            for x in range(2):
                if j < 4 or x == 1:
                    r_b_copy(h, j, x).start()
        for d in (2, 6):
            r_p(h, d).wait_recv()
        for c in r_a(h):
            c.wait_recv()
        for j, d in ((0, 2), (1, 6)):
            for i in range(2):
                t = term(h, d, i) + r_a1[h, j, i].astype(F32)
                if i == j:
                    t = t + r_a2[h, j].astype(F32)
                s_b[h, j, 0, i] = t[:T].astype(B16)
                s_b[h, j, 1, i] = t[T:].astype(B16)
            for x in range(2):
                r_b_copy(h, j, x).start()

    def reduce_last(h):
        for j in (2, 3, 4, 0, 1):
            if j == 4:
                r_b_copy(h, 4, 1).wait_recv()
            else:
                rcopy(s_b.at[h, j], r_b.at[h, j], rb_s.at[h, j, 0], rb_r.at[h, j], xp).wait_recv()
        cs = pl.ds(h * HD if isinstance(h, int) else pl.multiple_of(h * HD, HD), HD)
        for i in range(2):
            t = acc[h, 0, i, 0:T, :]
            for j in range(5):
                for x in range(2):
                    if j < 4 or x == 1:
                        t = t + r_b[h, j, x, i].astype(F32)
            if i == 0:
                dk_ref[:, cs] = (t * SCALE).astype(B16)
            else:
                dv_ref[:, cs] = t.astype(B16)

    cc = SCALE * LOG2E

    def score_tile(h, j):
        s_, e = j // 4, j % 4
        js = pl.ds(j * 256, 256)
        kk = jnp.concatenate([kv[h, s_, 0, 2 * e:2 * e + 2].reshape(256, HD), mk[js, :]], axis=1)
        for r in range(R // C1):
            rs = pl.ds(r * C1, C1)
            s = dot(kk, qa[h, rs, :], NT)
            m = jnp.max(jnp.max(s.reshape(32, 8, C1), axis=0), axis=0, keepdims=True)
            p = jnp.exp2((s - m) * cc)
            p_sc[js, rs] = p
            m_sc[j:j + 1, rs] = m
            l_sc[j:j + 1, rs] = jnp.sum(jnp.sum(p.reshape(32, 8, C1), axis=0), axis=0, keepdims=True)

    def score_end():
        m = m_sc[...]
        c = jnp.exp2((m - jnp.max(m, axis=0, keepdims=True)) * cc)
        sc[...] = c * (1.0 / jnp.sum(c * l_sc[...], axis=0, keepdims=True))

    def key_tile(h, t):
        d = ORDER[t]
        w = jnp.concatenate([p_sc[pl.ds(s_ * HALF + d * 128, 128), :] * sc[s_ * 4 + d // 2:s_ * 4 + d // 2 + 1, :] for s_ in range(2)], axis=0)
        vt = jnp.concatenate([jnp.concatenate([kv[h, s_, 1, d].reshape(128, HD) for s_ in range(2)], axis=0), ones], axis=1)
        dp = dot(vt, ga[h], NT)
        ds_ = (w * dp).astype(B16)
        pv = dot(w.astype(B16), ga[h, :, :HD])
        pk = dot(ds_, qa[h, :, :HD])
        ds_sc[h, d] = ds_
        for i, a in enumerate((pk, pv)):
            sp_p[h, d, i] = a[:128].astype(B16)
            acc[h, d, i] = a[128:]
        r_p(h, d).start()

    def finish_queries(h):
        kt = jnp.concatenate([kv[h, s_, 0, d].reshape(128, HD) for d in range(NZ) for s_ in range(2)], axis=0).T
        for r in range(R // 256):
            dq = (dot(kt, ds_sc[h, :, :, r * 256:(r + 1) * 256].reshape(NK, 256)) * SCALE).T.astype(B16)
            for e in range(4):
                c0 = (h * G + r * 4 + e) * HD
                dq_v[:, c0:c0 + HD] = dq[e * T:(e + 1) * T]

    def head(h):
        if h:
            gn_all(h).wait_recv()
            for j in range(0, 3):
                score_tile(h, j)
            if h > 1:
                reduce_last(h - 2)
            if h == 1:
                ring(2, 4)
                ring(3, 3)
            for j in range(3, 8):
                score_tile(h, j)
            score_end()
        key_tile(h, 0)
        if h == 0:
            ring(1, 3)
            ring(2, 2)
            ring(3, 1)
        key_tile(h, 1)
        key_tile(h, 2)
        if h:
            reduce_relay(h - 1)
        key_tile(h, 3)
        key_tile(h, 4)
        key_tile(h, 5)
        key_tile(h, 6)
        if h == 0:
            ring(1, 4)
            ring(2, 3)
            ring(3, 2)
        if h == 1:
            ring(3, 4)
        if h < KVH - 1:
            reduce_first(h)
        key_tile(h, 7)
        if h == KVH - 1:
            reduce_first(h)

    for h in range(KVH):
        prep_rows(h)
    pos_x().wait_recv()
    pos_b().start()
    make_mask(OWN)
    gather_relay(0)
    gather_send(1)
    gather_near(0)
    ring(1, 0)
    score_tile(0, 4)
    score_tile(0, 7)
    gather_last(0)
    gather_relay(1)
    gather_near(1)
    ring(2, 0)
    score_tile(0, 5)
    score_tile(0, 6)
    pos_b().wait_recv()
    make_mask(PREV)
    ring(1, 1)
    g_c(0, 0).wait_recv()
    g_c(0, 1).wait_recv()
    score_tile(0, 0)
    score_tile(0, 3)
    g_c(0, 2).wait_recv()
    score_tile(0, 1)
    score_tile(0, 2)
    score_end()
    gather_last(1)
    ring(1, 2)
    ring(2, 1)
    ring(3, 0)
    for n in range(3):
        g_c(1, n).wait_recv()

    for h in range(KVH):
        head(h)

    for h in range(KVH - 1):
        finish_queries(h)
    reduce_last(KVH - 2)
    reduce_relay(KVH - 1)
    finish_queries(KVH - 1)
    out = pltpu.make_async_copy(dq_v, dq_hbm, out_sem)
    out.start()
    reduce_last(KVH - 1)

    out.wait()
    pos_x().wait_send()
    pos_b().wait_send()
    for h in range(KVH):
        if h == 0:
            sent = [c for i in range(2) for c in g_a(i) + g_b(i) + [g_c(i, n) for n in range(3)]]
        else:
            sent = [gx(h), gn_all(h)] + [gu(h, s) for s in range(4)] + [gd(h, s) for s in range(4)]
        for c in sent + [r_p(h, d) for d in range(NZ)] + r_a(h):
            c.wait_send()
        for j in range(5):
            for x in range(2):
                if j < 4 or x == 1:
                    r_b_copy(h, j, x).wait_send()


def solution(mesh):
    nblk = mesh.shape["blk"]
    vm = pl.BlockSpec(memory_space=pltpu.VMEM)
    hb = pl.BlockSpec(memory_space=pl.ANY)
    dma = pltpu.SemaphoreType.DMA

    def local(q, k, v, o, g, pos):
        dt = q.dtype
        return pl.pallas_call(
            functools.partial(kernel, nblk),
            out_shape=(jax.ShapeDtypeStruct((T, QH * HD), dt), jax.ShapeDtypeStruct((T, KVH * HD), dt), jax.ShapeDtypeStruct((T, KVH * HD), dt)),
            in_specs=[hb, hb, hb, vm, vm, vm],
            out_specs=(hb, vm, vm),
            scratch_shapes=[
                pltpu.VMEM((T, QH * HD), B16), pltpu.VMEM((T, QH * HD), B16), pltpu.VMEM((T, QH * HD), B16), pltpu.VMEM((T, QH * HD), B16),
                pltpu.VMEM((KVH, 2, 2, NZ, 2, T, HD), B16),
                pltpu.VMEM((2, 2, 8, 128), jnp.int32),
                pltpu.VMEM((NK, 128), B16),
                pltpu.VMEM((KVH, R, 256), B16), pltpu.VMEM((KVH, R, 256), B16),
                pltpu.VMEM((KVH, NZ, 256, R), B16),
                pltpu.VMEM((NK, R), F32),
                pltpu.VMEM((8, R), F32), pltpu.VMEM((8, R), F32), pltpu.VMEM((8, R), F32),
                pltpu.VMEM((KVH, NZ, 2, 128, HD), F32),
                pltpu.VMEM((KVH, NZ, 2, 128, HD), B16), pltpu.VMEM((KVH, NZ, 2, 128, HD), B16),
                pltpu.VMEM((KVH, 2, 2, 128, HD), B16), pltpu.VMEM((KVH, 2, 128, HD), B16),
                pltpu.VMEM((KVH, 2, 2, 128, HD), B16), pltpu.VMEM((KVH, 2, 128, HD), B16),
                pltpu.VMEM((KVH, 5, 2, 2, T, HD), B16), pltpu.VMEM((KVH, 5, 2, 2, T, HD), B16),
                dma((3,)), dma,
                dma((KVH,)), dma((KVH,)), dma((KVH, 4)), dma((KVH, 4)), dma((KVH, 4)), dma((KVH, 4)), dma((KVH,)), dma((KVH,)),
                dma((2, 9)), dma((2, 3)), dma((2, 3)), dma((2, NZ)), dma((2, 3)),
                dma, dma, dma, dma,
                dma((KVH, NZ)), dma((KVH, NZ)),
                dma((KVH, 4)), dma((KVH, 4)), dma((KVH, 5, 2)), dma((KVH, 5)),
            ],
            compiler_params=pltpu.CompilerParams(collective_id=0, has_side_effects=True, vmem_limit_bytes=60 * 2 ** 20),
            cost_estimate=pl.CostEstimate(flops=12 * 10 ** 9, bytes_accessed=6 * 10 ** 6, transcendentals=9 * 10 ** 6),
        )(q, g, o, k, v, pos.reshape(1, T))

    spec = P(("blk", "uly"), None)
    return jax.shard_map(local, mesh=mesh, in_specs=(spec,) * 5 + (P(("blk", "uly")),), out_specs=(spec,) * 3, check_vma=False)
```

profile of v0, /device:TPU:57, one launch (start us, length us, event | category | flops | bytes accessed | tf_op | source)
XLA Modules:
  0.0 93.8 jit_solution(17420979557744745894)
XLA Ops:
  0.6 89.3 %shard_map.85 = (bf16[64,8192]{1,0:T(8,128)(2,1)}, bf16[64,512]{1,0:T(8,128)(2,1)}, bf16[64,512]{1,0:T(8,128)(2,1)}) custom-call(bf16[64,8192]{1,0:T(8,128)(2,1)} %q_hbm.1, bf16[64,8192]{1,0:T(8,128)(2,1)} %g_hbm.1, bf16[64,8192]{1,0:T(8,128)(2,1)} %o_hbm.1, bf16[64,512]{1,0:T(8,128)(2,1)} %k_ref.1, bf16[64,512]{1,0:T(8,128)(2,1)} %v_ref.1, s32[1,64]{1,0:T(1,128)} %bitcast.1), custom_call_target="tpu_custom_call" | custom-call | flops 12000000000 | bytes 6000000 | tf_op jit(solution)/shard_map/pallas_call | solution.py:422
  90.0 0.0 copy-start.1
  90.0 2.3 %copy.12 = bf16[64,8192]{1,0:T(8,128)(2,1)} copy(bf16[64,8192]{1,0:T(8,128)(2,1)} %get-tuple-element.6) | data formatting | bytes 2097152
  92.3 0.0 copy-done.1
  92.3 0.0 copy-start
  92.3 0.6 copy.13
  92.9 0.2 copy-done
  93.1 0.6 copy.14
Async XLA Ops:
  90.0 2.3 %copy-start.1 = (bf16[64,512]{1,0:T(8,128)(2,1)S(1)}, bf16[64,512]{1,0:T(8,128)(2,1)}, u32[]{:S(2)}) copy-start(bf16[64,512]{1,0:T(8,128)(2,1)} %get-tuple-element.7) | copy-start | bytes 196612
  92.3 0.9 copy-start
where the time goes:
time: 94 us; the launch traced here: 93.8 us
  Pallas kernels  89.3 us (95%)
  local copies, waits for them, and re-layouts  3.79 us (4%)
    pallas_call x1, Pallas kernels, local(): pl.pallas_call(functools.partial(kernel, nblk), out_shape=(jax.ShapeDtype...  89.3 us
    unnamed x7, local copies, waits for them, and re-layouts  3.79 us

commit v1 on v0

--- a/solution.py
+++ b/solution.py
@@ -220,7 +220,7 @@
         for c in r_a(h):
             c.start()
 
-    def reduce_relay(h):
+    def reduce_near(h):
         for d in (1, 7, 0):
             r_p(h, d).wait_recv()
         for j, d in ((2, 1), (3, 7), (4, 0)):
@@ -236,6 +236,8 @@
             for x in range(2):
                 if j < 4 or x == 1:
                     r_b_copy(h, j, x).start()
+
+    def reduce_far(h):
         for d in (2, 6):
             r_p(h, d).wait_recv()
         for c in r_a(h):
@@ -249,6 +251,10 @@
                 s_b[h, j, 1, i] = t[T:].astype(B16)
             for x in range(2):
                 r_b_copy(h, j, x).start()
+
+    def reduce_relay(h):
+        reduce_near(h)
+        reduce_far(h)
 
     def reduce_last(h):
         for j in (2, 3, 4, 0, 1):
@@ -386,10 +392,12 @@
     for h in range(KVH):
         head(h)
 
-    for h in range(KVH - 1):
-        finish_queries(h)
+    finish_queries(0)
+    finish_queries(1)
+    reduce_near(KVH - 1)
+    finish_queries(2)
+    reduce_far(KVH - 1)
     reduce_last(KVH - 2)
-    reduce_relay(KVH - 1)
     finish_queries(KVH - 1)
     out = pltpu.make_async_copy(dq_v, dq_hbm, out_sem)
     out.start()

time: 94 us -> 93.4 us (level)
  no operation moved by 1% of the time
where the time goes in v1:
time: 93.4 us; the launch traced here: 93.2 us
  Pallas kernels  88.7 us (95%)
  local copies, waits for them, and re-layouts  3.79 us (4%)
    pallas_call x1, Pallas kernels, local(): pl.pallas_call(functools.partial(kernel, nblk), out_shape=(jax.ShapeDtype...  88.7 us
    unnamed x7, local copies, waits for them, and re-layouts  3.79 us

profile of v1, /device:TPU:57, one launch (start us, length us, event | category | flops | bytes accessed | tf_op | source)
XLA Modules:
  0.0 93.2 jit_solution(14558136035952670877)
XLA Ops:
  0.6 88.7 %shard_map.85 = (bf16[64,8192]{1,0:T(8,128)(2,1)}, bf16[64,512]{1,0:T(8,128)(2,1)}, bf16[64,512]{1,0:T(8,128)(2,1)}) custom-call(bf16[64,8192]{1,0:T(8,128)(2,1)} %q_hbm.1, bf16[64,8192]{1,0:T(8,128)(2,1)} %g_hbm.1, bf16[64,8192]{1,0:T(8,128)(2,1)} %o_hbm.1, bf16[64,512]{1,0:T(8,128)(2,1)} %k_ref.1, bf16[64,512]{1,0:T(8,128)(2,1)} %v_ref.1, s32[1,64]{1,0:T(1,128)} %bitcast.1), custom_call_target="tpu_custom_call" | custom-call | flops 12000000000 | bytes 6000000 | tf_op jit(solution)/shard_map/pallas_call | solution.py:430
  89.4 0.0 copy-start.1
  89.4 2.3 %copy.12 = bf16[64,8192]{1,0:T(8,128)(2,1)} copy(bf16[64,8192]{1,0:T(8,128)(2,1)} %get-tuple-element.6) | data formatting | bytes 2097152
  91.7 0.0 copy-done.1
  91.7 0.0 copy-start
  91.7 0.6 copy.13
  92.3 0.2 copy-done
  92.5 0.6 copy.14
Async XLA Ops:
  89.4 2.3 %copy-start.1 = (bf16[64,512]{1,0:T(8,128)(2,1)S(1)}, bf16[64,512]{1,0:T(8,128)(2,1)}, u32[]{:S(2)}) copy-start(bf16[64,512]{1,0:T(8,128)(2,1)} %get-tuple-element.7) | copy-start | bytes 196612
  91.7 0.9 copy-start
